TPU v7x, 512 devices: a whole 4x8x8 slice. The times are simulated.
512 devices in a mesh: row: 16 (over y, core), col: 32 (over x, z).
Axes of the slice: x: 4, y: 8, z: 8, core: 2. Of those that a mesh axis runs over, the one named last changes fastest.
Arguments:
- points: float32 [64, 32768], P(None, ('row', 'col')), may hold values from -6 to 6
- lengthscale: float32 [64], replicated, may hold values from 2 to 8
- noise: float32 [32768], P(('row', 'col')), may hold values from 0.5 to 4
- iterate: float32 [16, 32768], P(None, ('row', 'col')), may hold values from -6 to 6
- residual: float32 [16, 32768], P(None, ('row', 'col')), may hold values from -6 to 6
- direction: float32 [16, 32768], P(None, ('row', 'col')), may hold values from -6 to 6
Outputs:
- new_iterate: float32 [16, 32768], P(None, ('row', 'col'))
- new_residual: float32 [16, 32768], P(None, ('row', 'col'))
- new_direction: float32 [16, 32768], P(None, ('row', 'col'))
All inputs are finite; a program needn't handle non-finite values.
Results may differ from a plain program's by a relative error of at most 0.004.
Values may be sent and summed in bfloat16 or wider, within the bound.
A program may use at most 64 MiB of HBM per device.

v0:
```python
import jax
import jax.numpy as jnp
from jax import lax
from jax.sharding import PartitionSpec as P


def matern(rows_z, cols_z):
    sq_rows = jnp.sum(rows_z * rows_z, axis=0)
    sq_cols = jnp.sum(cols_z * cols_z, axis=0)
    inner = lax.dot_general(
        rows_z,
        cols_z,
        (((0,), (0,)), ((), ())),
        precision=lax.Precision.HIGHEST,
        preferred_element_type=jnp.float32,
    )
    dist2 = jnp.maximum(sq_rows[:, None] + sq_cols[None, :] - 2.0 * inner, 0.0)
    scaled = jnp.sqrt(5.0 * dist2)
    return ((1.0 + scaled + scaled * scaled / 3.0) * jnp.exp(-scaled)).astype(jnp.bfloat16)


def image_part(piece, other_z, other_dir):
    kern = matern(piece, other_z)
    return lax.dot_general(
        other_dir, kern, (((1,), (1,)), ((), ())), preferred_element_type=jnp.float32
    )


def on_device(points, lengthscale, noise, iterate, residual, direction):
    scaled = points / lengthscale[:, None]
    dir_half = direction.astype(jnp.bfloat16)
    col_points = lax.all_gather(scaled, "row", axis=1, tiled=True)
    col_dir = lax.all_gather(dir_half, "row", axis=1, tiled=True)
    partial_sum = image_part(lax.all_gather(scaled, "col", axis=1, tiled=True), col_points, col_dir)
    kernel_image = lax.psum_scatter(partial_sum, "col", scatter_dimension=1, tiled=True)
    image = kernel_image + noise[None, :] * direction
    norm_local = jnp.sum(residual * residual, axis=1)
    curv_local = jnp.sum(direction * image, axis=1)
    norm_now, curv = lax.psum((norm_local, curv_local), ("row", "col"))
    alpha = norm_now / curv
    new_residual = residual - alpha[:, None] * image
    norm_next = lax.psum(jnp.sum(new_residual * new_residual, axis=1), ("row", "col"))
    new_iterate = iterate + alpha[:, None] * direction
    new_direction = new_residual + (norm_next / norm_now)[:, None] * direction
    return (new_iterate, new_residual, new_direction)


def solution(mesh):
    placed = (
        P(None, ("row", "col")),
        P(),
        P(("row", "col")),
        P(None, ("row", "col")),
        P(None, ("row", "col")),
        P(None, ("row", "col")),
    )
    return jax.shard_map(
        on_device,
        mesh=mesh,
        in_specs=placed,
        out_specs=(P(None, ("row", "col")), P(None, ("row", "col")), P(None, ("row", "col"))),
        check_vma=False,
    )
```

profile of v0, /device:TPU:1, one launch (start us, length us, event | category | flops | bytes accessed | tf_op | source)
XLA Modules:
  0.0 530.2 jit_solution(3267959373855155288)
XLA Ops:
  7.2 0.0 reduce-scatter.4.cloned.1.call-start
  7.2 0.8 copy.10
  8.0 0.7 broadcast_divide_fusion
  8.7 44.7 %all_gather.9 = f32[64,2048]{0,1:T(8,128)S(1)} all-gather(f32[64,64]{0,1:T(8,128)S(1)} %broadcast_divide_fusion), channel_id=1, replica_groups=mesh['row'=16,'col'=32] {'col'}, dimensions={1}, use_global_device_ids=true | all-gather | bytes 540672 | tf_op jit(solution)/shard_map/all_gather | solution.py:34
  53.4 32.0 %all_gather.10 = f32[64,1024]{0,1:T(8,128)S(1)} all-gather(f32[64,64]{0,1:T(8,128)S(1)} %broadcast_divide_fusion), channel_id=1, replica_groups=mesh['row'=16,'col'=32] {'row'}, dimensions={1}, use_global_device_ids=true | all-gather | bytes 278528 | tf_op jit(solution)/shard_map/all_gather | solution.py:32
  85.4 0.3 multiply_reduce_fusion
  85.8 0.2 multiply_reduce_fusion.1
  86.0 0.7 convert_bitcast_fusion
  86.7 15.1 %all-gather = bf16[16,64,16]{1,2,0:T(8,128)(2,1)S(1)} all-gather(bf16[1,64,16]{1,2,0:T(8,128)(2,1)S(1)} %convert_bitcast_fusion), channel_id=1, replica_groups=mesh['row'=16,'col'=32] {'row'}, dimensions={0}, use_global_device_ids=true | all-gather | bytes 34816 | tf_op jit(solution)/shard_map/all_gather | solution.py:33
  101.8 0.1 reshape.13
  101.9 12.0 %multiply_convert_fusion = bf16[2048,1024]{1,0:T(8,128)(2,1)S(1)} fusion(f32[64,2048]{0,1:T(8,128)S(1)} %all_gather.9, f32[64,1024]{0,1:T(8,128)S(1)} %all_gather.10, f32[1024]{0:T(1024)S(1)} %multiply_reduce_fusion.1, f32[2048]{0:T(1024)S(1)} %multiply_reduce_fusion), kind=kOutput, calls=%fused_computation | convolution fusion | flops 1635778560 | bytes 4993024 | tf_op jit(solution)/shard_map/dot_general | solution.py:10
  113.9 0.0 copy-start
  113.9 0.0 copy-start.1
  113.9 0.0 copy-start.4
  113.9 0.0 copy-start.3
  113.9 1.2 convolution_bitcast_fusion
  115.1 1.3 copy.12
  116.5 0.0 reduce-scatter.4.cloned.1.call-update
  116.5 208.8 %reduce-scatter.4.cloned.1.call-done = f32[64,16]{1,0:T(8,128)} async-done(((f32[2048,16]{1,0:T(8,128)}), f32[64,16]{1,0:T(8,128)}) %reduce-scatter.4.cloned.1.call-update) | async-done | bytes 4112
  325.3 0.8 copy.13
  326.1 0.0 copy-done
  326.1 0.0 copy-done.1
  326.1 0.0 copy-done.4
  326.1 0.1 multiply_reduce_fusion.3
  326.2 100.5 %all-reduce = (f32[16]{0:T(128)S(1)}, f32[16]{0:T(128)S(1)}) all-reduce(f32[16]{0:T(128)S(1)} %get-tuple-element.9, f32[16]{0:T(128)S(1)} %get-tuple-element.8), channel_id=1, replica_groups=mesh['row'=16,'col'=32] {'row','col'}, use_global_device_ids=true, to_apply=%region_1.0 | all-reduce | flops 32 | bytes 256 | tf_op jit(solution)/shard_map/psum | solution.py:39
  426.7 0.0 copy-done.3
  426.7 0.8 multiply_reduce_fusion.2
  427.5 0.0 copy-start.2
  427.5 95.2 %psum.23 = f32[16]{0:T(128)S(1)} all-reduce(f32[16]{0:T(128)S(1)} %get-tuple-element.5), channel_id=1, replica_groups=mesh['row'=16,'col'=32] {'row','col'}, use_global_device_ids=true, to_apply=%region_8.0 | all-reduce | flops 16 | bytes 128 | tf_op jit(solution)/shard_map/psum | solution.py:42
  522.7 0.7 multiply_add_fusion
  523.4 0.0 copy-done.2
  (3 shorter events, 0.0 us)
Async XLA Ops:
  7.2 318.1 %reduce-scatter.4.cloned.1.call-start = ((), (), s32[]{:S(2)}) async-start(), calls=%async_computation.1 | async-start | bytes 1081344
  113.9 212.2 %copy-start = (f32[16,64]{1,0:T(8,128)S(1)}, f32[16,64]{1,0:T(8,128)}, u32[]{:S(2)}) copy-start(f32[16,64]{1,0:T(8,128)} %param.11) | copy-start | bytes 12292
  113.9 212.2 %copy-start.1 = (f32[16,64]{1,0:T(8,128)S(1)}, f32[16,64]{1,0:T(8,128)}, u32[]{:S(2)}) copy-start(f32[16,64]{1,0:T(8,128)} %param.10) | copy-start | bytes 12292
  113.9 212.2 %copy-start.4 = (f32[64]{0:T(128)S(1)}, f32[64]{0:T(128)}, u32[]{:S(2)}) copy-start(f32[64]{0:T(128)} %param.8) | copy-start | bytes 772
  113.9 312.8 %copy-start.3 = (f32[16,64]{1,0:T(8,128)S(1)}, f32[16,64]{1,0:T(8,128)}, u32[]{:S(2)}) copy-start(f32[16,64]{1,0:T(8,128)} %param.9) | copy-start | bytes 12292
  427.5 95.9 %copy-start.2 = (f32[16,64]{1,0:T(8,128)}, f32[16,64]{1,0:T(8,128)S(1)}, u32[]{:S(2)}) copy-start(f32[16,64]{1,0:T(8,128)S(1)} %get-tuple-element.6) | copy-start | bytes 12292
Sparse Core Ops, SparseCore 0:
  116.6 208.6 reduce-scatter.3
where the time goes:
time: 531 us; the launch traced here: 530 us
  blocking collectives  287 us (54%)
  waiting for transfers between devices  209 us (39%)
  between operations  14.1 us (3%)
  matrix products  13.2 us (2%)
    unnamed x2, waiting for transfers between devices  209 us
    psum x1, blocking collectives, on_device(): norm_now, curv = lax.psum((norm_local, curv_local), ('row', 'col'))  100 us
    psum x1, blocking collectives, on_device(): lax.psum(jnp.sum(new_residual * new_residual, axis=1), ('row', 'col'))  95.2 us
    all_gather x1, blocking collectives, on_device(): lax.all_gather(scaled, 'col', axis=1, tiled=True)  44.7 us
    all_gather x1, blocking collectives, on_device(): col_points = lax.all_gather(scaled, 'row', axis=1, tiled=True)  32 us
    all_gather x1, blocking collectives, on_device(): col_dir = lax.all_gather(dir_half, 'row', axis=1, tiled=True)  15.1 us
    dot_general x1, matrix products, matern(): lax.dot_general(rows_z, cols_z, (((0,), (0,)), ((), ())), precision=lax.P...  12 us
  transfers between devices with their start and end apart: 1, of which 1 were waited for; matrix products, arithmetic and copies ran while one was open for 0% of the time, Pallas kernels for 0%

commit v1 on v0

v1 whole, which is shorter than its diff:
```python
import functools
import math

import jax
import jax.numpy as jnp
from jax import lax
from jax.experimental import pallas as pl
from jax.experimental.pallas import tpu as pltpu
from jax.sharding import PartitionSpec as P

MESH = pl.DeviceIdType.MESH
F32 = jnp.float32
BF16 = jnp.bfloat16
FEAT = 64
RHS = 16
PTS = 64
NX = 4
LOG2E = math.log2(math.e)
SCALE = math.sqrt(5.0) * LOG2E
TINY = 1e-30


def half_lanes(shape):
    return lax.broadcasted_iota(jnp.int32, shape, 1) < 64


def swap(x):
    return pltpu.roll(x, 64, 1)


def split3(s):
    a = s.astype(BF16).astype(F32)
    b = (s - a).astype(BF16).astype(F32)
    c = (s - a - b).astype(BF16).astype(F32)
    return a, b, c


def kernel(
    nrow, ncol,
    points, scale, noise, iterate, residual, direction,
    new_iterate, new_residual, new_direction,
    cbuf, rbuf, rmat, amat, prod, psend, pbuf, stat_a, stat_b, tot_a, tot_b,
    c_send, c_recv, r_send, r_recv, p_send, p_recv, a_send, a_recv, b_send, b_recv,
):
    nz = ncol // NX
    row, col = lax.axis_index("row"), lax.axis_index("col")
    x, z = col // nz, col % nz

    def row_peer(d):
        return (lax.rem(row + d, nrow), col)

    def col_peer(dx, dz):
        return (row, lax.rem(x + dx, NX) * nz + lax.rem(z + dz, nz))

    dzs = [0]
    for k in range(1, nz // 2 + 1):
        dzs += [k] if 2 * k == nz else [k, nz - k]
    col_offsets = [(g, dx) for g in range(nz) for dx in range(NX) if (g, dx) != (0, 0)]

    barrier = pltpu.get_barrier_semaphore()
    for d in range(1, nrow):
        pl.semaphore_signal(barrier, inc=1, device_id=row_peer(d), device_id_type=MESH)
    for g, dx in reversed(col_offsets):
        pl.semaphore_signal(barrier, inc=1, device_id=col_peer(dx, dzs[g]), device_id_type=MESH)

    ls_col = jnp.transpose(jnp.broadcast_to(scale[...], (FEAT, FEAT)))
    zf = points[...] / ls_col * SCALE
    hi = zf.astype(BF16).astype(F32)
    lo = (zf - hi).astype(BF16).astype(F32)
    rbuf[0] = jnp.concatenate([hi, lo], axis=1).astype(BF16)
    sq = jnp.sum((hi + lo) * (hi + lo), axis=0, keepdims=True)
    s1, s2, s3 = split3(sq)
    one = jnp.ones_like(sq)
    ext = jnp.concatenate([s1, s2, s3, one, one, one, one * 0, one * 0], axis=0)
    pad = jnp.zeros((FEAT - 8, PTS), F32)
    hi_t = jnp.transpose(hi)
    lo_t = jnp.transpose(lo)
    ext_t = jnp.transpose(jnp.concatenate([ext, pad], axis=0))
    cbuf[0, 0, 0:64, :] = jnp.concatenate([hi_t, lo_t], axis=1).astype(BF16)
    own_dir = direction[...]
    packed = jnp.concatenate([own_dir, ext_t[0:16]], axis=1)
    lane16 = lax.broadcasted_iota(jnp.int32, (16, 128), 1)
    for a in range(1, 4):
        piece = jnp.concatenate([ext_t[16 * a:16 * a + 16], jnp.zeros((16, 64), F32)], axis=1)
        packed = jnp.where((lane16 >= 64 + 8 * a) & (lane16 < 72 + 8 * a), pltpu.roll(piece, 64 + 8 * a, 1), packed)
    cbuf[0, 0, 64:80, :] = packed.astype(BF16)

    pl.semaphore_wait(barrier, nrow - 1 + ncol - 1)

    sends = []

    def send(src, dst, ssem, rsem, peer):
        copy = pltpu.make_async_remote_copy(
            src_ref=src, dst_ref=dst, send_sem=ssem, recv_sem=rsem,
            device_id=peer, device_id_type=MESH)
        copy.start()
        sends.append(copy)

    def arrived(ref, sem):
        pltpu.make_async_copy(ref, ref, sem).wait()

    for d in range(1, nrow):
        send(rbuf.at[0], rbuf.at[d], r_send.at[d], r_recv, row_peer(d))
    for i, (g, dx) in enumerate(reversed(col_offsets)):
        send(cbuf.at[0, 0], cbuf.at[g, dx], c_send.at[i], c_recv.at[g], col_peer(dx, dzs[g]))

    arrived(rbuf.at[pl.ds(1, nrow - 1)], r_recv)
    left = half_lanes((FEAT, 128))
    sub = lax.broadcasted_iota(jnp.int32, (64, 128), 0)
    for pair in range(nrow // 2):
        c0 = rbuf[2 * pair].astype(F32)
        c1 = rbuf[2 * pair + 1].astype(F32)
        h = jnp.where(left, c0, swap(c1))
        l = jnp.where(left, swap(c0), c1)
        t1, t2, t3 = split3(jnp.sum((h + l) * (h + l), axis=0, keepdims=True))
        e = jnp.where(sub < 3, 1.0, jnp.where(sub == 3, t1, jnp.where(sub == 4, t2, jnp.where(sub == 5, t3, 0.0))))
        lanes = slice(128 * pair, 128 * pair + 128)
        h2 = (-2.0 * h).astype(BF16)
        rmat[0:64, lanes] = h2
        rmat[64:128, lanes] = h2
        rmat[128:192, lanes] = (-2.0 * l).astype(BF16)
        rmat[192:256, lanes] = e.astype(BF16)

    prod[...] = jnp.zeros_like(prod)
    npts = nrow * PTS
    width = 256
    left16 = half_lanes((16, 128))

    def group(g, carry):
        @pl.when(g == 0)
        def _():
            arrived(cbuf.at[0, pl.ds(1, NX - 1)], c_recv.at[0])

        @pl.when(g > 0)
        def _():
            arrived(cbuf.at[g], c_recv.at[g])

        dirs = []
        for dx in range(NX):
            tail = cbuf[g, dx, 64:80, :].astype(F32)
            dirs.append(tail)
            for a in range(4):
                rows = slice(64 * dx + 16 * a, 64 * dx + 16 * a + 16)
                body = cbuf[g, dx, 16 * a:16 * a + 16, :]
                amat[rows, 0:128] = body
                shifted = tail if a == 0 else pltpu.roll(tail, 128 - 8 * a, 1)
                amat[rows, 128:256] = jnp.where(left16, body.astype(F32), shifted).astype(BF16)
        dgrp = jnp.concatenate(
            [jnp.where(left16, dirs[0], swap(dirs[1])), jnp.where(left16, dirs[2], swap(dirs[3]))], axis=1).astype(BF16)
        for it in range(npts // width):
            lanes = slice(width * it, width * it + width)
            dist = jnp.dot(amat[...], rmat[:, lanes], preferred_element_type=F32)
            dist = jnp.maximum(dist, TINY)
            v = dist * lax.rsqrt(dist)
            w = v * (1.0 / (LOG2E * math.sqrt(3.0))) + math.sqrt(0.75)
            kern = ((w * w + 0.25) * jnp.exp2(-v)).astype(BF16)
            prod[:, lanes] += jnp.dot(dgrp, kern, preferred_element_type=F32)
        return carry

    lax.fori_loop(0, nz, group, 0)

    left8 = half_lanes((8, 128))
    for pair in range(nrow // 2):
        top = prod[0:8, 128 * pair:128 * pair + 128]
        bottom = prod[8:16, 128 * pair:128 * pair + 128]
        psend[2 * pair] = jnp.where(left8, top, swap(bottom))
        psend[2 * pair + 1] = jnp.where(left8, swap(top), bottom)
    for d in range(1, nrow):
        send(psend.at[d], pbuf.at[d], p_send.at[d], p_recv, row_peer(nrow - d))
    pbuf[0] = psend[0]
    res = residual[...]
    arrived(pbuf.at[pl.ds(1, nrow - 1)], p_recv)
    total = jnp.sum(pbuf[...], axis=0)
    image = jnp.concatenate([total, swap(total)], axis=0)[:, 0:64] + noise[...] * own_dir

    def norm(a, b):
        return jnp.sum(a * b, axis=1, keepdims=True)

    stats = jnp.where(
        lane16 == 0, norm(res, res),
        jnp.where(lane16 == 1, norm(own_dir, image),
                  jnp.where(lane16 == 2, norm(res, image),
                            jnp.where(lane16 == 3, norm(image, image), 0.0))))
    tot_a[...] = stats[0:8] + swap(stats[8:16])
    for d in range(1, nrow):
        send(tot_a, stat_a.at[d], a_send.at[d], a_recv, row_peer(d))
    stat_a[0] = tot_a[...]
    arrived(stat_a.at[pl.ds(1, nrow - 1)], a_recv)
    tot_b[...] = jnp.sum(stat_a[...], axis=0)
    for i, (g, dx) in enumerate(reversed(col_offsets)):
        send(tot_b, stat_b.at[g * NX + dx], b_send.at[i], b_recv, col_peer(dx, dzs[g]))
    stat_b[0] = tot_b[...]
    arrived(stat_b.at[pl.ds(1, ncol - 1)], b_recv)
    total = jnp.sum(stat_b[...], axis=0)
    total = jnp.concatenate([total, swap(total)], axis=0)
    rr, curv, cross, square = (total[:, k:k + 1] for k in range(4))
    alpha = rr / curv
    rr_new = jnp.maximum(rr - 2.0 * (alpha * cross) + alpha * (alpha * square), 0.0)
    beta = rr_new / rr
    fresh = res - alpha * image
    new_iterate[...] = iterate[...] + alpha * own_dir
    new_residual[...] = fresh
    new_direction[...] = fresh + beta * own_dir
    for copy in sends:
        copy.wait_send()


def solution(mesh):
    nrow, ncol = mesh.shape["row"], mesh.shape["col"]
    nz = ncol // NX
    spread = P(None, ("row", "col"))
    placed = (spread, P(), P(("row", "col")), spread, spread, spread)
    vmem = pl.BlockSpec(memory_space=pltpu.VMEM)
    dma = pltpu.SemaphoreType.DMA
    shape = jax.ShapeDtypeStruct((RHS, PTS), F32)

    step = pl.pallas_call(
        functools.partial(kernel, nrow, ncol),
        out_shape=(shape, shape, shape),
        in_specs=[vmem] * 6,
        out_specs=(vmem,) * 3,
        scratch_shapes=[
            pltpu.VMEM((nz, NX, 80, 128), BF16),
            pltpu.VMEM((nrow, 64, 128), BF16),
            pltpu.VMEM((256, nrow * PTS), BF16),
            pltpu.VMEM((256, 256), BF16),
            pltpu.VMEM((RHS, nrow * PTS), F32),
            pltpu.VMEM((nrow, 8, 128), F32),
            pltpu.VMEM((nrow, 8, 128), F32),
            pltpu.VMEM((nrow, 8, 128), F32),
            pltpu.VMEM((ncol, 8, 128), F32),
            pltpu.VMEM((8, 128), F32),
            pltpu.VMEM((8, 128), F32),
            dma((ncol,)), dma((nz,)), dma((nrow,)), dma,
            dma((nrow,)), dma, dma((nrow,)), dma, dma((ncol,)), dma,
        ],
        compiler_params=pltpu.CompilerParams(
            collective_id=0, has_side_effects=True, vmem_limit_bytes=32 * 1024 * 1024),
        name="cg_step",
    )

    def on_device(points, lengthscale, noise, iterate, residual, direction):
        return step(points, lengthscale.reshape(1, FEAT), noise.reshape(1, PTS), iterate, residual, direction)

    return jax.shard_map(
        on_device, mesh=mesh, in_specs=placed, out_specs=(spread, spread, spread), check_vma=False)
```

time: 531 us -> 63.8 us (0.12)
  blocking collectives: 287 us -> 0 us
  waiting for transfers between devices: 209 us -> 0 us
  Pallas kernels: 0 us -> 57.5 us
  between operations: 14.1 us -> 0.66 us
  matrix products: 13.2 us -> 0 us
    unnamed x2 -> x0, waiting for transfers between devices: 209 us -> none
    psum x2 -> x0, blocking collectives: 196 us -> none  [the longest x1 100 us: on_device(): norm_now, curv = lax.psum((norm_local, curv_local), ('row', 'col'))]
    all_gather x3 -> x0, blocking collectives: 91.8 us -> none  [the longest x1 44.7 us: on_device(): lax.all_gather(scaled, 'col', axis=1, tiled=True)]
    pallas_call x0 -> x1, Pallas kernels: none -> 57.5 us  [on_device(): step(points, lengthscale.reshape(1, FEAT), noise.reshape(1, PTS), iterate...]
    dot_general x2 -> x0, matrix products: 13.2 us -> none  [the longest x1 12 us: matern(): lax.dot_general(rows_z, cols_z, (((0,), (0,)), ((), ())), precision=lax.P...]
  transfers between devices with their start and end apart: 1 -> 0, of which waited for: 1 -> 0; matrix products, arithmetic and copies ran while one was open for 0% -> 0% of each run, Pallas kernels for 0% -> 0%
where the time goes in v1:
time: 63.8 us; the launch traced here: 63.5 us
  Pallas kernels  57.5 us (90%)
  local copies, waits for them, and re-layouts  5.3 us (8%)
  between operations  0.66 us (1%)
    pallas_call x1, Pallas kernels, on_device(): step(points, lengthscale.reshape(1, FEAT), noise.reshape(1, PTS), iterate...  57.5 us
    unnamed x15, local copies, waits for them, and re-layouts  5.3 us

profile of v1, /device:TPU:1, one launch (start us, length us, event | category | flops | bytes accessed | tf_op | source)
XLA Modules:
  0.0 63.5 jit_solution(17518453912002928674)
XLA Ops:
  0.6 0.0 copy-start.4
  0.6 0.0 copy-start.5
  0.7 0.6 %copy-done.4 = f32[64]{0:T(128)S(1)} copy-done((f32[64]{0:T(128)S(1)}, f32[64]{0:T(128)}, u32[]{:S(2)}) %copy-start.4) | copy-done | bytes 280
  1.3 0.0 copy-done.5
  1.3 0.0 copy-start
  1.3 0.8 %copy-done = f32[64,64]{1,0:T(8,128)S(1)} copy-done((f32[64,64]{1,0:T(8,128)S(1)}, f32[64,64]{1,0:T(8,128)}, u32[]{:S(2)}) %copy-start) | copy-done | bytes 16408
  2.1 0.0 copy-start.1
  2.1 0.7 %copy-done.1 = f32[16,64]{1,0:T(8,128)S(1)} copy-done((f32[16,64]{1,0:T(8,128)S(1)}, f32[16,64]{1,0:T(8,128)}, u32[]{:S(2)}) %copy-start.1) | copy-done | bytes 4120
  2.8 0.0 copy-start.2
  2.8 0.7 %copy-done.2 = f32[16,64]{1,0:T(8,128)S(1)} copy-done((f32[16,64]{1,0:T(8,128)S(1)}, f32[16,64]{1,0:T(8,128)}, u32[]{:S(2)}) %copy-start.2) | copy-done | bytes 4120
  3.5 0.0 copy-start.3
  3.5 0.7 %copy-done.3 = f32[16,64]{1,0:T(8,128)S(1)} copy-done((f32[16,64]{1,0:T(8,128)S(1)}, f32[16,64]{1,0:T(8,128)}, u32[]{:S(2)}) %copy-start.3) | copy-done | bytes 4120
  4.2 57.5 %cg_step.1 = (f32[16,64]{1,0:T(8,128)S(1)}, f32[16,64]{1,0:T(8,128)S(1)}, f32[16,64]{1,0:T(8,128)S(1)}) custom-call(f32[64,64]{1,0:T(8,128)S(1)} %copy-done, f32[1,64]{1,0:T(1,128)S(1)} %bitcast.2, f32[1,64]{1,0:T(1,128)S(1)} %bitcast.3, f32[16,64]{1,0:T(8,128)S(1)} %copy-done.1, f32[16,64]{1,0:T(8,128)S(1)} %copy-done.2, f32[16,64]{1,0:T(8,128)S(1)} %copy-done.3), custom_call_target="tpu_custom_call" | custom-call | tf_op jit(solution)/shard_map/cg_step/pallas_call | solution.py:243
  61.7 0.6 copy.12
  62.3 0.6 copy.13
  62.9 0.6 copy.14
Async XLA Ops:
  0.6 0.7 %copy-start.4 = (f32[64]{0:T(128)S(1)}, f32[64]{0:T(128)}, u32[]{:S(2)}) copy-start(f32[64]{0:T(128)} %param.7) | copy-start | bytes 772
  0.6 0.7 %copy-start.5 = (f32[64]{0:T(128)S(1)}, f32[64]{0:T(128)}, u32[]{:S(2)}) copy-start(f32[64]{0:T(128)} %param.8) | copy-start | bytes 772
  1.3 0.8 %copy-start = (f32[64,64]{1,0:T(8,128)S(1)}, f32[64,64]{1,0:T(8,128)}, u32[]{:S(2)}) copy-start(f32[64,64]{1,0:T(8,128)} %points.1) | copy-start | bytes 49156
  2.1 0.7 %copy-start.1 = (f32[16,64]{1,0:T(8,128)S(1)}, f32[16,64]{1,0:T(8,128)}, u32[]{:S(2)}) copy-start(f32[16,64]{1,0:T(8,128)} %iterate.1) | copy-start | bytes 12292
  2.8 0.7 %copy-start.2 = (f32[16,64]{1,0:T(8,128)S(1)}, f32[16,64]{1,0:T(8,128)}, u32[]{:S(2)}) copy-start(f32[16,64]{1,0:T(8,128)} %residual.1) | copy-start | bytes 12292
  3.5 0.7 %copy-start.3 = (f32[16,64]{1,0:T(8,128)S(1)}, f32[16,64]{1,0:T(8,128)}, u32[]{:S(2)}) copy-start(f32[16,64]{1,0:T(8,128)} %direction.1) | copy-start | bytes 12292

commit v2 on v1

v2 whole, which is shorter than its diff:
```python
import functools
import math

import jax
import jax.numpy as jnp
from jax import lax
from jax.experimental import pallas as pl
from jax.experimental.pallas import tpu as pltpu
from jax.sharding import PartitionSpec as P

MESH = pl.DeviceIdType.MESH
F32 = jnp.float32
BF16 = jnp.bfloat16
FEAT = 64
RHS = 16
PTS = 64
NX = 4
LOG2E = math.log2(math.e)
SCALE = math.sqrt(5.0) * LOG2E
TINY = 1e-30


def half_lanes(shape):
    return lax.broadcasted_iota(jnp.int32, shape, 1) < 64


def swap(x):
    return pltpu.roll(x, 64, 1)


def split3(s):
    a = s.astype(BF16).astype(F32)
    b = (s - a).astype(BF16).astype(F32)
    c = (s - a - b).astype(BF16).astype(F32)
    return a, b, c


def kernel(
    nrow, ncol,
    points_hbm, scale_hbm, noise_hbm, residual_hbm, direction_hbm,
    image_out, alpha_out, beta_out,
    points, scale, noise, residual, direction,
    cbuf, rbuf, rmat, amat, kbuf, prod, psend, pbuf, stat_a, stat_b, tot_a, tot_b,
    in_sem, c_send, z_recv, x_recv, r_send, y_recv, k_recv,
    p_send, p_recv, a_send, a_recv, b_send, b_recv,
):
    nz, ny = ncol // NX, nrow // 2
    row, col = lax.axis_index("row"), lax.axis_index("col")
    x, z, y, k = col // nz, col % nz, row // 2, row % 2

    def device(dx=0, dy=0, dz=0, dk=0):
        return (
            lax.rem(y + dy, ny) * 2 + lax.rem(k + dk, 2),
            lax.rem(x + dx, NX) * nz + lax.rem(z + dz, nz),
        )

    def near_first(n):
        steps = []
        for s in range(1, n // 2 + 1):
            steps += [s] if 2 * s == n else [s, n - s]
        return steps

    zs, ys, xs = near_first(nz), near_first(ny), near_first(NX)
    far_zs, far_ys, far_xs = zs[::-1], ys[::-1], xs[::-1]
    row_steps = [(dy, dk) for dy in far_ys + [0] for dk in (1, 0) if (dy, dk) != (0, 0)]
    col_steps = [(dz, dx) for dz in far_zs + [0] for dx in far_xs + [0] if (dz, dx) != (0, 0)]

    loads = []
    for i, (src, dst) in enumerate((
            (points_hbm, points), (scale_hbm, scale), (direction_hbm, direction),
            (noise_hbm, noise), (residual_hbm, residual))):
        copy = pltpu.make_async_copy(src, dst, in_sem.at[i])
        copy.start()
        loads.append(copy)

    barrier = pltpu.get_barrier_semaphore()
    greeted = (
        [device(dz=s) for s in far_zs] + [device(dy=s) for s in far_ys]
        + [device(dx=s) for s in far_xs] + [device(dk=1)])
    for peer in greeted:
        pl.semaphore_signal(barrier, inc=1, device_id=peer, device_id_type=MESH)

    for copy in loads[:3]:
        copy.wait()
    ls_col = jnp.transpose(jnp.broadcast_to(scale[...], (FEAT, FEAT)))
    zf = points[...] / ls_col * SCALE
    hi = zf.astype(BF16).astype(F32)
    lo = (zf - hi).astype(BF16).astype(F32)
    rbuf[0, 0] = jnp.concatenate([hi, lo], axis=1).astype(BF16)
    sq = jnp.sum((hi + lo) * (hi + lo), axis=0, keepdims=True)
    s1, s2, s3 = split3(sq)
    one = jnp.ones_like(sq)
    ext = jnp.concatenate([s1, s2, s3, one, one, one, one * 0, one * 0], axis=0)
    pad = jnp.zeros((FEAT - 8, PTS), F32)
    hi_t = jnp.transpose(hi)
    lo_t = jnp.transpose(lo)
    ext_t = jnp.transpose(jnp.concatenate([ext, pad], axis=0))
    cbuf[0, 0, 0:64, :] = jnp.concatenate([hi_t, lo_t], axis=1).astype(BF16)
    own_dir = direction[...]
    packed = jnp.concatenate([own_dir, ext_t[0:16]], axis=1)
    lane16 = lax.broadcasted_iota(jnp.int32, (16, 128), 1)
    for a in range(1, 4):
        piece = jnp.concatenate([ext_t[16 * a:16 * a + 16], jnp.zeros((16, 64), F32)], axis=1)
        packed = jnp.where((lane16 >= 64 + 8 * a) & (lane16 < 72 + 8 * a), pltpu.roll(piece, 64 + 8 * a, 1), packed)
    cbuf[0, 0, 64:80, :] = packed.astype(BF16)

    pl.semaphore_wait(barrier, len(greeted))

    sends = []

    def send(src, dst, ssem, rsem, peer):
        copy = pltpu.make_async_remote_copy(
            src_ref=src, dst_ref=dst, send_sem=ssem, recv_sem=rsem,
            device_id=peer, device_id_type=MESH)
        copy.start()
        sends.append(copy)

    def arrived(ref, sem):
        pltpu.make_async_copy(ref, ref, sem).wait()

    def to_x(dz):
        for dx in far_xs:
            send(cbuf.at[dz, 0], cbuf.at[dz, dx], c_send.at[dz, dx], x_recv.at[dz], device(dx=dx))

    def to_core(dy):
        send(rbuf.at[dy, 0], rbuf.at[dy, 1], r_send.at[dy, 1], k_recv.at[dy], device(dk=1))

    for dz, dy in zip(far_zs, far_ys):
        send(cbuf.at[0, 0], cbuf.at[dz, 0], c_send.at[dz, 0], z_recv.at[dz], device(dz=dz))
        send(rbuf.at[0, 0], rbuf.at[dy, 0], r_send.at[dy, 0], y_recv.at[dy], device(dy=dy))
    to_x(0)
    to_core(0)
    for dz, dy in zip(zs, ys):
        arrived(cbuf.at[dz, 0], z_recv.at[dz])
        to_x(dz)
        arrived(rbuf.at[dy, 0], y_recv.at[dy])
        to_core(dy)

    left = half_lanes((FEAT, 128))
    sub = lax.broadcasted_iota(jnp.int32, (64, 128), 0)
    for dy in [0] + ys:
        arrived(rbuf.at[dy, 1], k_recv.at[dy])
        c0 = rbuf[dy, 0].astype(F32)
        c1 = rbuf[dy, 1].astype(F32)
        h = jnp.where(left, c0, swap(c1))
        l = jnp.where(left, swap(c0), c1)
        t1, t2, t3 = split3(jnp.sum((h + l) * (h + l), axis=0, keepdims=True))
        e = jnp.where(sub < 3, 1.0, jnp.where(sub == 3, t1, jnp.where(sub == 4, t2, jnp.where(sub == 5, t3, 0.0))))
        lanes = slice(128 * dy, 128 * dy + 128)
        h2 = (-2.0 * h).astype(BF16)
        rmat[0:64, lanes] = h2
        rmat[64:128, lanes] = h2
        rmat[128:192, lanes] = (-2.0 * l).astype(BF16)
        rmat[192:256, lanes] = e.astype(BF16)

    left16 = half_lanes((16, 128))
    width = 256
    blocks = [slice(width * i, width * i + width) for i in range(nrow * PTS // width)]

    def operands(dz):
        dirs = []
        for dx in range(NX):
            tail = cbuf[dz, dx, 64:80, :].astype(F32)
            dirs.append(tail)
            for a in range(4):
                rows = slice(64 * dx + 16 * a, 64 * dx + 16 * a + 16)
                body = cbuf[dz, dx, 16 * a:16 * a + 16, :]
                amat[rows, 0:128] = body
                shifted = tail if a == 0 else pltpu.roll(tail, 128 - 8 * a, 1)
                amat[rows, 128:256] = jnp.where(left16, body.astype(F32), shifted).astype(BF16)
        return jnp.concatenate(
            [jnp.where(left16, dirs[0], swap(dirs[1])), jnp.where(left16, dirs[2], swap(dirs[3]))], axis=1).astype(BF16)

    def entries(lanes):
        dist = jnp.dot(amat[...], rmat[:, lanes], preferred_element_type=F32)
        dist = jnp.maximum(dist, TINY)
        v = dist * lax.rsqrt(dist)
        w = v * (1.0 / (LOG2E * math.sqrt(3.0))) + math.sqrt(0.75)
        return ((w * w + 0.25) * jnp.exp2(-v)).astype(BF16)

    before = None
    for n, dz in enumerate([0] + zs):
        arrived(cbuf.at[dz, pl.ds(1, NX - 1)], x_recv.at[dz])
        dgrp = operands(dz)
        for lanes in blocks:
            kern = entries(lanes)
            if n == 1:
                prod[:, lanes] = jnp.dot(before, kbuf[(n - 1) % 2, :, lanes], preferred_element_type=F32)
            elif n > 1:
                prod[:, lanes] += jnp.dot(before, kbuf[(n - 1) % 2, :, lanes], preferred_element_type=F32)
            kbuf[n % 2, :, lanes] = kern
        before = dgrp
    for lanes in blocks:
        prod[:, lanes] += jnp.dot(before, kbuf[(nz - 1) % 2, :, lanes], preferred_element_type=F32)

    left8 = half_lanes((8, 128))
    for dy in far_ys + [0]:
        top = prod[0:8, 128 * dy:128 * dy + 128]
        bottom = prod[8:16, 128 * dy:128 * dy + 128]
        psend[dy, 0] = jnp.where(left8, top, swap(bottom))
        psend[dy, 1] = jnp.where(left8, swap(top), bottom)
    for dy, dk in row_steps:
        send(psend.at[dy, dk], pbuf.at[dy * 2 + dk], p_send.at[dy, dk], p_recv, device(dy=ny - dy, dk=dk))
    pbuf[0] = psend[0, 0]
    loads[3].wait()
    loads[4].wait()
    res = residual[...]
    arrived(pbuf.at[pl.ds(1, nrow - 1)], p_recv)
    total = jnp.sum(pbuf[...], axis=0)
    image = jnp.concatenate([total, swap(total)], axis=0)[:, 0:64] + noise[...] * own_dir
    image_out[...] = image

    def norm(a, b):
        return jnp.sum(a * b, axis=1, keepdims=True)

    stats = jnp.where(
        lane16 == 0, norm(res, res),
        jnp.where(lane16 == 1, norm(own_dir, image),
                  jnp.where(lane16 == 2, norm(res, image),
                            jnp.where(lane16 == 3, norm(image, image), 0.0))))
    tot_a[...] = stats[0:8] + swap(stats[8:16])
    for dy, dk in row_steps:
        send(tot_a, stat_a.at[dy * 2 + dk], a_send.at[dy, dk], a_recv, device(dy=dy, dk=dk))
    stat_a[0] = tot_a[...]
    arrived(stat_a.at[pl.ds(1, nrow - 1)], a_recv)
    tot_b[...] = jnp.sum(stat_a[...], axis=0)
    for dz, dx in col_steps:
        send(tot_b, stat_b.at[dz * NX + dx], b_send.at[dz, dx], b_recv, device(dz=dz, dx=dx))
    stat_b[0] = tot_b[...]
    arrived(stat_b.at[pl.ds(1, ncol - 1)], b_recv)
    total = jnp.sum(stat_b[...], axis=0)
    total = jnp.concatenate([total, swap(total)], axis=0)
    rr, curv, cross, square = (total[:, i:i + 1] for i in range(4))
    alpha = rr / curv
    rr_new = jnp.maximum(rr - 2.0 * (alpha * cross) + alpha * (alpha * square), 0.0)
    beta = rr_new / rr
    alpha_out[...] = jnp.broadcast_to(alpha, (RHS, PTS))
    beta_out[...] = jnp.broadcast_to(beta, (RHS, PTS))
    for copy in sends:
        copy.wait_send()


def solution(mesh):
    nrow, ncol = mesh.shape["row"], mesh.shape["col"]
    nz, ny = ncol // NX, nrow // 2
    spread = P(None, ("row", "col"))
    placed = (spread, P(), P(("row", "col")), spread, spread, spread)
    vmem = pl.BlockSpec(memory_space=pltpu.VMEM)
    dma = pltpu.SemaphoreType.DMA
    shape = jax.ShapeDtypeStruct((RHS, PTS), F32)

    step = pl.pallas_call(
        functools.partial(kernel, nrow, ncol),
        out_shape=(shape, shape, shape),
        in_specs=[pl.BlockSpec(memory_space=pltpu.HBM)] * 5,
        out_specs=(vmem,) * 3,
        scratch_shapes=[
            pltpu.VMEM((FEAT, PTS), F32),
            pltpu.VMEM((1, FEAT), F32),
            pltpu.VMEM((1, PTS), F32),
            pltpu.VMEM((RHS, PTS), F32),
            pltpu.VMEM((RHS, PTS), F32),
            pltpu.VMEM((nz, NX, 80, 128), BF16),
            pltpu.VMEM((ny, 2, 64, 128), BF16),
            pltpu.VMEM((256, nrow * PTS), BF16),
            pltpu.VMEM((256, 256), BF16),
            pltpu.VMEM((2, 256, nrow * PTS), BF16),
            pltpu.VMEM((RHS, nrow * PTS), F32),
            pltpu.VMEM((ny, 2, 8, 128), F32),
            pltpu.VMEM((nrow, 8, 128), F32),
            pltpu.VMEM((nrow, 8, 128), F32),
            pltpu.VMEM((ncol, 8, 128), F32),
            pltpu.VMEM((8, 128), F32),
            pltpu.VMEM((8, 128), F32),
            dma((5,)), dma((nz, NX)), dma((nz,)), dma((nz,)), dma((ny, 2)), dma((ny,)), dma((ny,)),
            dma((ny, 2)), dma, dma((ny, 2)), dma, dma((nz, NX)), dma,
        ],
        compiler_params=pltpu.CompilerParams(
            collective_id=0, has_side_effects=True, vmem_limit_bytes=60 * 1024 * 1024),
        name="cg_step",
    )

    def on_device(points, lengthscale, noise, iterate, residual, direction):
        image, alpha, beta = step(
            points, lengthscale.reshape(1, FEAT), noise.reshape(1, PTS), residual, direction)
        fresh = residual - alpha * image
        return iterate + alpha * direction, fresh, fresh + beta * direction

    return jax.shard_map(
        on_device, mesh=mesh, in_specs=placed, out_specs=(spread, spread, spread), check_vma=False)
```

time: 63.8 us -> 49.6 us (0.78)
  Pallas kernels: 57.5 us -> 47.3 us
  local copies, waits for them, and re-layouts: 5.3 us -> 0.01 us
  other arithmetic: 0 us -> 1.34 us
    pallas_call x1, Pallas kernels: 57.5 us -> 47.3 us  [on_device(): step(points, lengthscale.reshape(1, FEAT), noise.reshape(1, PTS), residua...]
    unnamed x15 -> x6, local copies, waits for them, and re-layouts: 5.3 us -> 0.01 us
    add x0 -> x1, other arithmetic: none -> 1.34 us  [on_device(): return (iterate + alpha * direction, fresh, fresh + beta * direction)]
where the time goes in v2:
time: 49.6 us; the launch traced here: 49.3 us
  Pallas kernels  47.3 us (95%)
  other arithmetic  1.34 us (3%)
  between operations  0.69 us (1%)
    pallas_call x1, Pallas kernels, on_device(): step(points, lengthscale.reshape(1, FEAT), noise.reshape(1, PTS), residua...  47.3 us
    add x1, other arithmetic, on_device(): return (iterate + alpha * direction, fresh, fresh + beta * direction)  1.34 us

profile of v2, /device:TPU:1, one launch (start us, length us, event | category | flops | bytes accessed | tf_op | source)
XLA Modules:
  0.0 49.3 jit_solution(14040767138847559239)
XLA Ops:
  0.6 0.0 copy-start
  0.6 0.0 copy-start.1
  0.7 0.0 copy-start.2
  0.7 47.3 %cg_step.1 = (f32[16,64]{1,0:T(8,128)}, f32[16,64]{1,0:T(8,128)}, f32[16,64]{1,0:T(8,128)}) custom-call(f32[64,64]{1,0:T(8,128)} %points_hbm.1, f32[1,64]{1,0:T(1,128)} %bitcast.2, f32[1,64]{1,0:T(1,128)} %bitcast.3, f32[16,64]{1,0:T(8,128)} %residual_hbm.1, f32[16,64]{1,0:T(8,128)} %direction_hbm.1), custom_call_target="tpu_custom_call" | custom-call | tf_op jit(solution)/shard_map/cg_step/pallas_call | solution.py:284
  48.0 0.0 copy-done
  48.0 0.0 copy-done.1
  48.0 0.0 copy-done.2
  48.0 1.3 %multiply_add_fusion = (f32[16,64]{1,0:T(8,128)}, f32[16,64]{1,0:T(8,128)}, f32[16,64]{1,0:T(8,128)}) fusion(f32[16,64]{1,0:T(8,128)} %get-tuple-element.8, f32[16,64]{1,0:T(8,128)S(1)} %copy-done.1, f32[16,64]{1,0:T(8,128)S(1)} %copy-done, f32[16,64]{1,0:T(8,128)} %get-tuple-element.6, f32[16,64]{1,0:T(8,128)} %get-tuple-element.7, f32[16,64]{1,0:T(8,128)S(1)} %copy-done.2), kind=kLoop, calls=%fused_computation | loop fusion | flops 6144 | bytes 36864 | tf_op jit(solution)/shard_map/add | solution.py:287
Async XLA Ops:
  0.6 47.3 %copy-start = (f32[16,64]{1,0:T(8,128)S(1)}, f32[16,64]{1,0:T(8,128)}, u32[]{:S(2)}) copy-start(f32[16,64]{1,0:T(8,128)} %residual_hbm.1) | copy-start | bytes 12292
  0.6 47.3 %copy-start.1 = (f32[16,64]{1,0:T(8,128)S(1)}, f32[16,64]{1,0:T(8,128)}, u32[]{:S(2)}) copy-start(f32[16,64]{1,0:T(8,128)} %direction_hbm.1) | copy-start | bytes 12292
  0.7 47.3 %copy-start.2 = (f32[16,64]{1,0:T(8,128)S(1)}, f32[16,64]{1,0:T(8,128)}, u32[]{:S(2)}) copy-start(f32[16,64]{1,0:T(8,128)} %param.9) | copy-start | bytes 12292

commit v3 on v2

--- a/solution.py
+++ b/solution.py
@@ -16,8 +16,11 @@
 PTS = 64
 NX = 4
 LOG2E = math.log2(math.e)
-SCALE = math.sqrt(5.0) * LOG2E
+SCALE = math.sqrt(5.0)
 TINY = 1e-30
+Z_MAX = 3.0
+STEEP = 251.0 / Z_MAX
+LOW = 125.0
 
 
 def half_lanes(shape):
@@ -33,6 +36,17 @@
     b = (s - a).astype(BF16).astype(F32)
     c = (s - a - b).astype(BF16).astype(F32)
     return a, b, c
+
+
+def encode(z):
+    mag = jnp.exp2(jnp.abs(z) * STEEP - LOW)
+    return jnp.where(z < 0, -mag, mag).astype(BF16)
+
+
+def decode(code):
+    w = code.astype(F32)
+    z = (jnp.log2(jnp.abs(w)) + LOW) * (SCALE / STEEP)
+    return jnp.where(w < 0, -z, z)
 
 
 def kernel(
@@ -65,6 +79,13 @@
     row_steps = [(dy, dk) for dy in far_ys + [0] for dk in (1, 0) if (dy, dk) != (0, 0)]
     col_steps = [(dz, dx) for dz in far_zs + [0] for dx in far_xs + [0] if (dz, dx) != (0, 0)]
 
+    barrier = pltpu.get_barrier_semaphore()
+    greeted = (
+        [device(dz=s) for s in far_zs] + [device(dy=s) for s in far_ys]
+        + [device(dx=s) for s in far_xs] + [device(dk=1)])
+    for peer in greeted:
+        pl.semaphore_signal(barrier, inc=1, device_id=peer, device_id_type=MESH)
+
     loads = []
     for i, (src, dst) in enumerate((
             (points_hbm, points), (scale_hbm, scale), (direction_hbm, direction),
@@ -73,36 +94,31 @@
         copy.start()
         loads.append(copy)
 
-    barrier = pltpu.get_barrier_semaphore()
-    greeted = (
-        [device(dz=s) for s in far_zs] + [device(dy=s) for s in far_ys]
-        + [device(dx=s) for s in far_xs] + [device(dk=1)])
-    for peer in greeted:
-        pl.semaphore_signal(barrier, inc=1, device_id=peer, device_id_type=MESH)
-
     for copy in loads[:3]:
         copy.wait()
     ls_col = jnp.transpose(jnp.broadcast_to(scale[...], (FEAT, FEAT)))
-    zf = points[...] / ls_col * SCALE
+    code = encode(points[...] / ls_col)
+    zf = decode(code)
     hi = zf.astype(BF16).astype(F32)
     lo = (zf - hi).astype(BF16).astype(F32)
-    rbuf[0, 0] = jnp.concatenate([hi, lo], axis=1).astype(BF16)
+    code = code.astype(F32)
+    half = FEAT // 2
+    rbuf[0, 0] = jnp.concatenate([code[0:half], code[half:FEAT]], axis=1).astype(BF16)
     sq = jnp.sum((hi + lo) * (hi + lo), axis=0, keepdims=True)
     s1, s2, s3 = split3(sq)
     one = jnp.ones_like(sq)
     ext = jnp.concatenate([s1, s2, s3, one, one, one, one * 0, one * 0], axis=0)
     pad = jnp.zeros((FEAT - 8, PTS), F32)
-    hi_t = jnp.transpose(hi)
-    lo_t = jnp.transpose(lo)
+    code_t = jnp.transpose(code)
     ext_t = jnp.transpose(jnp.concatenate([ext, pad], axis=0))
-    cbuf[0, 0, 0:64, :] = jnp.concatenate([hi_t, lo_t], axis=1).astype(BF16)
+    cbuf[0, 0, 0:32, :] = jnp.concatenate([code_t[0:32], code_t[32:64]], axis=1).astype(BF16)
     own_dir = direction[...]
     packed = jnp.concatenate([own_dir, ext_t[0:16]], axis=1)
     lane16 = lax.broadcasted_iota(jnp.int32, (16, 128), 1)
     for a in range(1, 4):
         piece = jnp.concatenate([ext_t[16 * a:16 * a + 16], jnp.zeros((16, 64), F32)], axis=1)
         packed = jnp.where((lane16 >= 64 + 8 * a) & (lane16 < 72 + 8 * a), pltpu.roll(piece, 64 + 8 * a, 1), packed)
-    cbuf[0, 0, 64:80, :] = packed.astype(BF16)
+    cbuf[0, 0, 32:48, :] = packed.astype(BF16)
 
     pl.semaphore_wait(barrier, len(greeted))
 
@@ -130,23 +146,27 @@
         send(rbuf.at[0, 0], rbuf.at[dy, 0], r_send.at[dy, 0], y_recv.at[dy], device(dy=dy))
     to_x(0)
     to_core(0)
-    for dz, dy in zip(zs, ys):
+    def forward(dz, dy):
         arrived(cbuf.at[dz, 0], z_recv.at[dz])
         to_x(dz)
         arrived(rbuf.at[dy, 0], y_recv.at[dy])
         to_core(dy)
 
-    left = half_lanes((FEAT, 128))
+    near_ys = [0] + ys
+    left = half_lanes((FEAT // 2, 128))
     sub = lax.broadcasted_iota(jnp.int32, (64, 128), 0)
-    for dy in [0] + ys:
+
+    def row_operand(n):
+        dy = near_ys[n]
         arrived(rbuf.at[dy, 1], k_recv.at[dy])
-        c0 = rbuf[dy, 0].astype(F32)
-        c1 = rbuf[dy, 1].astype(F32)
-        h = jnp.where(left, c0, swap(c1))
-        l = jnp.where(left, swap(c0), c1)
+        c0 = decode(rbuf[dy, 0])
+        c1 = decode(rbuf[dy, 1])
+        full = jnp.concatenate([jnp.where(left, c0, swap(c1)), jnp.where(left, swap(c0), c1)], axis=0)
+        h = full.astype(BF16).astype(F32)
+        l = (full - h).astype(BF16).astype(F32)
         t1, t2, t3 = split3(jnp.sum((h + l) * (h + l), axis=0, keepdims=True))
         e = jnp.where(sub < 3, 1.0, jnp.where(sub == 3, t1, jnp.where(sub == 4, t2, jnp.where(sub == 5, t3, 0.0))))
-        lanes = slice(128 * dy, 128 * dy + 128)
+        lanes = slice(128 * n, 128 * n + 128)
         h2 = (-2.0 * h).astype(BF16)
         rmat[0:64, lanes] = h2
         rmat[64:128, lanes] = h2
@@ -156,51 +176,76 @@
     left16 = half_lanes((16, 128))
     width = 256
     blocks = [slice(width * i, width * i + width) for i in range(nrow * PTS // width)]
-
-    def operands(dz):
+    dirs_of = {}
+
+    def col_operand(dz):
+        arrived(cbuf.at[dz, pl.ds(1, NX - 1)], x_recv.at[dz])
         dirs = []
         for dx in range(NX):
-            tail = cbuf[dz, dx, 64:80, :].astype(F32)
+            tail = cbuf[dz, dx, 32:48, :].astype(F32)
             dirs.append(tail)
+            full = decode(cbuf[dz, dx, 0:32, :])
+            high = full.astype(BF16).astype(F32)
+            low = full - high
             for a in range(4):
                 rows = slice(64 * dx + 16 * a, 64 * dx + 16 * a + 16)
-                body = cbuf[dz, dx, 16 * a:16 * a + 16, :]
-                amat[rows, 0:128] = body
-                shifted = tail if a == 0 else pltpu.roll(tail, 128 - 8 * a, 1)
-                amat[rows, 128:256] = jnp.where(left16, body.astype(F32), shifted).astype(BF16)
-        return jnp.concatenate(
+                part = slice(16 * (a % 2), 16 * (a % 2) + 16)
+                h, l = high[part], low[part]
+                h, l = (h, swap(l)) if a < 2 else (swap(h), l)
+                extra = tail if a == 0 else pltpu.roll(tail, 128 - 8 * a, 1)
+                amat[dz, rows, 0:128] = jnp.where(left16, h, l).astype(BF16)
+                amat[dz, rows, 128:256] = jnp.where(left16, h, extra).astype(BF16)
+        dirs_of[dz] = jnp.concatenate(
             [jnp.where(left16, dirs[0], swap(dirs[1])), jnp.where(left16, dirs[2], swap(dirs[3]))], axis=1).astype(BF16)
 
-    def entries(lanes):
-        dist = jnp.dot(amat[...], rmat[:, lanes], preferred_element_type=F32)
+    pending = []
+    begun = set()
+
+    def product():
+        dz, i = pending.pop()
+        part = jnp.dot(dirs_of[dz], kbuf[dz, :, blocks[i]], preferred_element_type=F32)
+        prod[:, blocks[i]] = prod[:, blocks[i]] + part if i in begun else part
+        begun.add(i)
+
+    def entries(dz, i):
+        dist = jnp.dot(amat[dz], rmat[:, blocks[i]], preferred_element_type=F32)
         dist = jnp.maximum(dist, TINY)
-        v = dist * lax.rsqrt(dist)
-        w = v * (1.0 / (LOG2E * math.sqrt(3.0))) + math.sqrt(0.75)
-        return ((w * w + 0.25) * jnp.exp2(-v)).astype(BF16)
-
-    before = None
-    for n, dz in enumerate([0] + zs):
-        arrived(cbuf.at[dz, pl.ds(1, NX - 1)], x_recv.at[dz])
-        dgrp = operands(dz)
-        for lanes in blocks:
-            kern = entries(lanes)
-            if n == 1:
-                prod[:, lanes] = jnp.dot(before, kbuf[(n - 1) % 2, :, lanes], preferred_element_type=F32)
-            elif n > 1:
-                prod[:, lanes] += jnp.dot(before, kbuf[(n - 1) % 2, :, lanes], preferred_element_type=F32)
-            kbuf[n % 2, :, lanes] = kern
-        before = dgrp
-    for lanes in blocks:
-        prod[:, lanes] += jnp.dot(before, kbuf[(nz - 1) % 2, :, lanes], preferred_element_type=F32)
+        root = dist * lax.rsqrt(dist)
+        kern = ((dist * (1.0 / 3.0) + 1.0 + root) * jnp.exp2(root * -LOG2E)).astype(BF16)
+        if pending:
+            product()
+        kbuf[dz, :, blocks[i]] = kern
+        pending.append((dz, i))
 
     left8 = half_lanes((8, 128))
-    for dy in far_ys + [0]:
-        top = prod[0:8, 128 * dy:128 * dy + 128]
-        bottom = prod[8:16, 128 * dy:128 * dy + 128]
-        psend[dy, 0] = jnp.where(left8, top, swap(bottom))
-        psend[dy, 1] = jnp.where(left8, swap(top), bottom)
-    for dy, dk in row_steps:
-        send(psend.at[dy, dk], pbuf.at[dy * 2 + dk], p_send.at[dy, dk], p_recv, device(dy=ny - dy, dk=dk))
+
+    def scatter(i):
+        for n in (2 * i + 1, 2 * i):
+            dy = near_ys[n]
+            top = prod[0:8, 128 * n:128 * n + 128]
+            bottom = prod[8:16, 128 * n:128 * n + 128]
+            psend[dy, 0] = jnp.where(left8, top, swap(bottom))
+            psend[dy, 1] = jnp.where(left8, swap(top), bottom)
+            for dk in (1, 0):
+                if (dy, dk) != (0, 0):
+                    send(psend.at[dy, dk], pbuf.at[dy * 2 + dk], p_send.at[dy, dk], p_recv, device(dy=ny - dy, dk=dk))
+
+    for dz, dy in zip(zs, ys):
+        forward(dz, dy)
+    for n in range(8):
+        row_operand(n)
+    for dz in [0] + zs[:-1]:
+        col_operand(dz)
+        for i in range(4):
+            entries(dz, i)
+    col_operand(zs[-1])
+    for i in (3, 2, 1, 0):
+        entries(zs[-1], i)
+        if i < 3:
+            scatter(i + 1)
+    product()
+    scatter(0)
+
     pbuf[0] = psend[0, 0]
     loads[3].wait()
     loads[4].wait()
@@ -260,11 +305,11 @@
             pltpu.VMEM((1, PTS), F32),
             pltpu.VMEM((RHS, PTS), F32),
             pltpu.VMEM((RHS, PTS), F32),
-            pltpu.VMEM((nz, NX, 80, 128), BF16),
-            pltpu.VMEM((ny, 2, 64, 128), BF16),
+            pltpu.VMEM((nz, NX, 48, 128), BF16),
+            pltpu.VMEM((ny, 2, 32, 128), BF16),
             pltpu.VMEM((256, nrow * PTS), BF16),
-            pltpu.VMEM((256, 256), BF16),
-            pltpu.VMEM((2, 256, nrow * PTS), BF16),
+            pltpu.VMEM((nz, 256, 256), BF16),
+            pltpu.VMEM((nz, 256, nrow * PTS), BF16),
             pltpu.VMEM((RHS, nrow * PTS), F32),
             pltpu.VMEM((ny, 2, 8, 128), F32),
             pltpu.VMEM((nrow, 8, 128), F32),
@@ -276,7 +321,7 @@
             dma((ny, 2)), dma, dma((ny, 2)), dma, dma((nz, NX)), dma,
         ],
         compiler_params=pltpu.CompilerParams(
-            collective_id=0, has_side_effects=True, vmem_limit_bytes=60 * 1024 * 1024),
+            collective_id=0, has_side_effects=True, vmem_limit_bytes=539 * 1024 * 1024 // 10),
         name="cg_step",
     )
 

time: 49.6 us -> 45.7 us (0.921)
  Pallas kernels: 47.3 us -> 43.5 us
  other arithmetic: 1.34 us -> 0.61 us
  local copies, waits for them, and re-layouts: 0.01 us -> 0.67 us
    pallas_call x1, Pallas kernels: 47.3 us -> 43.5 us  [on_device(): step(points, lengthscale.reshape(1, FEAT), noise.reshape(1, PTS), residua...]
    add x1, other arithmetic: 1.34 us -> 0.61 us  [on_device(): return (iterate + alpha * direction, fresh, fresh + beta * direction)]
    unnamed x6 -> x10, local copies, waits for them, and re-layouts: 0.01 us -> 0.67 us
where the time goes in v3:
time: 45.7 us; the launch traced here: 45.4 us
  Pallas kernels  43.5 us (95%)
  between operations  0.68 us (1%)
  local copies, waits for them, and re-layouts  0.67 us (1%)
  other arithmetic  0.61 us (1%)
    pallas_call x1, Pallas kernels, on_device(): step(points, lengthscale.reshape(1, FEAT), noise.reshape(1, PTS), residua...  43.5 us

profile of v3, /device:TPU:1, one launch (start us, length us, event | category | flops | bytes accessed | tf_op | source)
XLA Modules:
  0.0 45.4 jit_solution(12761101145935389896)
XLA Ops:
  0.6 0.0 copy-start
  0.6 0.0 copy-start.1
  0.7 0.6 %copy-done = f32[64]{0:T(128)S(1)} copy-done((f32[64]{0:T(128)S(1)}, f32[64]{0:T(128)}, u32[]{:S(2)}) %copy-start) | copy-done | bytes 280
  1.3 0.0 copy-done.1
  1.3 0.0 copy-start.2
  1.3 0.0 copy-start.3
  1.3 0.0 copy-start.4
  1.3 43.5 %cg_step.1 = (f32[16,64]{1,0:T(8,128)S(1)}, f32[16,64]{1,0:T(8,128)S(1)}, f32[16,64]{1,0:T(8,128)S(1)}) custom-call(f32[64,64]{1,0:T(8,128)} %points_hbm.1, f32[1,64]{1,0:T(1,128)S(1)} %bitcast.2, f32[1,64]{1,0:T(1,128)S(1)} %bitcast.3, f32[16,64]{1,0:T(8,128)} %residual_hbm.1, f32[16,64]{1,0:T(8,128)} %direction_hbm.1), custom_call_target="tpu_custom_call" | custom-call | tf_op jit(solution)/shard_map/cg_step/pallas_call | solution.py:329
  44.8 0.0 copy-done.2
  44.8 0.0 copy-done.3
  44.8 0.0 copy-done.4
  44.8 0.6 %multiply_add_fusion = (f32[16,64]{1,0:T(8,128)}, f32[16,64]{1,0:T(8,128)}, f32[16,64]{1,0:T(8,128)}) fusion(f32[16,64]{1,0:T(8,128)S(1)} %get-tuple-element.8, f32[16,64]{1,0:T(8,128)S(1)} %copy-done.3, f32[16,64]{1,0:T(8,128)S(1)} %copy-done.2, f32[16,64]{1,0:T(8,128)S(1)} %get-tuple-element.6, f32[16,64]{1,0:T(8,128)S(1)} %get-tuple-element.7, ...), kind=kLoop, calls=%fused_computation | loop fusion | flops 6144 | bytes 36864 | tf_op jit(solution)/shard_map/add | solution.py:332
Async XLA Ops:
  0.6 0.7 %copy-start = (f32[64]{0:T(128)S(1)}, f32[64]{0:T(128)}, u32[]{:S(2)}) copy-start(f32[64]{0:T(128)} %param.7) | copy-start | bytes 772
  0.6 0.7 %copy-start.1 = (f32[64]{0:T(128)S(1)}, f32[64]{0:T(128)}, u32[]{:S(2)}) copy-start(f32[64]{0:T(128)} %param.8) | copy-start | bytes 772
  1.3 43.5 %copy-start.2 = (f32[16,64]{1,0:T(8,128)S(1)}, f32[16,64]{1,0:T(8,128)}, u32[]{:S(2)}) copy-start(f32[16,64]{1,0:T(8,128)} %residual_hbm.1) | copy-start | bytes 12292
  1.3 43.5 %copy-start.3 = (f32[16,64]{1,0:T(8,128)S(1)}, f32[16,64]{1,0:T(8,128)}, u32[]{:S(2)}) copy-start(f32[16,64]{1,0:T(8,128)} %direction_hbm.1) | copy-start | bytes 12292
  1.3 43.5 %copy-start.4 = (f32[16,64]{1,0:T(8,128)S(1)}, f32[16,64]{1,0:T(8,128)}, u32[]{:S(2)}) copy-start(f32[16,64]{1,0:T(8,128)} %param.9) | copy-start | bytes 12292

commit v4 on v3

--- a/solution.py
+++ b/solution.py
@@ -258,24 +258,38 @@
     def norm(a, b):
         return jnp.sum(a * b, axis=1, keepdims=True)
 
-    stats = jnp.where(
-        lane16 == 0, norm(res, res),
-        jnp.where(lane16 == 1, norm(own_dir, image),
-                  jnp.where(lane16 == 2, norm(res, image),
-                            jnp.where(lane16 == 3, norm(image, image), 0.0))))
-    tot_a[...] = stats[0:8] + swap(stats[8:16])
-    for dy, dk in row_steps:
-        send(tot_a, stat_a.at[dy * 2 + dk], a_send.at[dy, dk], a_recv, device(dy=dy, dk=dk))
+    sub16s = lax.broadcasted_iota(jnp.int32, (16, 128), 0)
+    stats8 = jnp.where(
+        lane16 == 4 * sub16s, norm(res, res),
+        jnp.where(lane16 == 4 * sub16s + 1, norm(own_dir, image),
+                  jnp.where(lane16 == 4 * sub16s + 2, norm(res, image),
+                            jnp.where(lane16 == 4 * sub16s + 3, norm(image, image), 0.0))))
+
+    def hops(step, n):
+        return min(step, n - step)
+
+    every = sorted(
+        ((dx, dy, dz) for dx in range(NX) for dy in range(ny) for dz in range(nz) if dx + dy + dz > 0),
+        key=lambda s: -(hops(s[0], NX) + hops(s[1], ny) + hops(s[2], nz)))
+    tot_a[...] = jnp.sum(stats8, axis=0, keepdims=True)
+    for n, (dx, dy, dz) in enumerate(every):
+        pltpu.make_async_remote_copy(
+            src_ref=tot_a, dst_ref=stat_a.at[n + 1], send_sem=a_send, recv_sem=a_recv,
+            device_id=device(dx=dx, dy=dy, dz=dz), device_id_type=MESH).start()
     stat_a[0] = tot_a[...]
-    arrived(stat_a.at[pl.ds(1, nrow - 1)], a_recv)
+    others = stat_a.at[pl.ds(1, len(every))]
+    arrived(others, a_recv)
     tot_b[...] = jnp.sum(stat_a[...], axis=0)
-    for dz, dx in col_steps:
-        send(tot_b, stat_b.at[dz * NX + dx], b_send.at[dz, dx], b_recv, device(dz=dz, dx=dx))
-    stat_b[0] = tot_b[...]
-    arrived(stat_b.at[pl.ds(1, ncol - 1)], b_recv)
-    total = jnp.sum(stat_b[...], axis=0)
-    total = jnp.concatenate([total, swap(total)], axis=0)
-    rr, curv, cross, square = (total[:, i:i + 1] for i in range(4))
+    send(tot_b, stat_b, b_send, b_recv, device(dk=1))
+    arrived(others, a_send)
+    arrived(stat_b, b_recv)
+    row1 = tot_b[...] + stat_b[...]
+    rows8 = lax.broadcasted_iota(jnp.int32, (8, 128), 0)
+    spread8 = jnp.broadcast_to(row1, (16, 128))
+    sub16 = lax.broadcasted_iota(jnp.int32, (16, 128), 0)
+    def pick(i):
+        return jnp.sum(jnp.where(lane16 == 4 * sub16 + i, spread8, 0.0), axis=1, keepdims=True)
+    rr, curv, cross, square = (pick(i) for i in range(4))
     alpha = rr / curv
     rr_new = jnp.maximum(rr - 2.0 * (alpha * cross) + alpha * (alpha * square), 0.0)
     beta = rr_new / rr
@@ -313,12 +327,12 @@
             pltpu.VMEM((RHS, nrow * PTS), F32),
             pltpu.VMEM((ny, 2, 8, 128), F32),
             pltpu.VMEM((nrow, 8, 128), F32),
-            pltpu.VMEM((nrow, 8, 128), F32),
-            pltpu.VMEM((ncol, 8, 128), F32),
-            pltpu.VMEM((8, 128), F32),
-            pltpu.VMEM((8, 128), F32),
+            pltpu.VMEM((nrow * ncol // 2, 1, 128), F32),
+            pltpu.VMEM((1, 128), F32),
+            pltpu.VMEM((1, 128), F32),
+            pltpu.VMEM((1, 128), F32),
             dma((5,)), dma((nz, NX)), dma((nz,)), dma((nz,)), dma((ny, 2)), dma((ny,)), dma((ny,)),
-            dma((ny, 2)), dma, dma((ny, 2)), dma, dma((nz, NX)), dma,
+            dma((ny, 2)), dma, dma, dma, dma, dma,
         ],
         compiler_params=pltpu.CompilerParams(
             collective_id=0, has_side_effects=True, vmem_limit_bytes=539 * 1024 * 1024 // 10),

time: 45.7 us -> 44.8 us (0.980)
  Pallas kernels: 43.5 us -> 42.6 us
    pallas_call x1, Pallas kernels: 43.5 us -> 42.6 us  [on_device(): step(points, lengthscale.reshape(1, FEAT), noise.reshape(1, PTS), residua...]
where the time goes in v4:
time: 44.8 us; the launch traced here: 44.6 us
  Pallas kernels  42.6 us (95%)
  between operations  0.68 us (2%)
  local copies, waits for them, and re-layouts  0.67 us (1%)
  other arithmetic  0.61 us (1%)
    pallas_call x1, Pallas kernels, on_device(): step(points, lengthscale.reshape(1, FEAT), noise.reshape(1, PTS), residua...  42.6 us

profile of v4, /device:TPU:1, one launch (start us, length us, event | category | flops | bytes accessed | tf_op | source)
XLA Modules:
  0.0 44.6 jit_solution(14842553879878886948)
XLA Ops:
  0.6 0.0 copy-start
  0.6 0.0 copy-start.1
  0.7 0.6 %copy-done = f32[64]{0:T(128)S(1)} copy-done((f32[64]{0:T(128)S(1)}, f32[64]{0:T(128)}, u32[]{:S(2)}) %copy-start) | copy-done | bytes 280
  1.3 0.0 copy-done.1
  1.3 0.0 copy-start.2
  1.3 0.0 copy-start.3
  1.3 0.0 copy-start.4
  1.3 42.6 %cg_step.1 = (f32[16,64]{1,0:T(8,128)S(1)}, f32[16,64]{1,0:T(8,128)S(1)}, f32[16,64]{1,0:T(8,128)S(1)}) custom-call(f32[64,64]{1,0:T(8,128)} %points_hbm.1, f32[1,64]{1,0:T(1,128)S(1)} %bitcast.2, f32[1,64]{1,0:T(1,128)S(1)} %bitcast.3, f32[16,64]{1,0:T(8,128)} %residual_hbm.1, f32[16,64]{1,0:T(8,128)} %direction_hbm.1), custom_call_target="tpu_custom_call" | custom-call | tf_op jit(solution)/shard_map/cg_step/pallas_call | solution.py:343
  43.9 0.0 copy-done.2
  43.9 0.0 copy-done.3
  43.9 0.0 copy-done.4
  43.9 0.6 %multiply_add_fusion = (f32[16,64]{1,0:T(8,128)}, f32[16,64]{1,0:T(8,128)}, f32[16,64]{1,0:T(8,128)}) fusion(f32[16,64]{1,0:T(8,128)S(1)} %get-tuple-element.8, f32[16,64]{1,0:T(8,128)S(1)} %copy-done.3, f32[16,64]{1,0:T(8,128)S(1)} %copy-done.2, f32[16,64]{1,0:T(8,128)S(1)} %get-tuple-element.6, f32[16,64]{1,0:T(8,128)S(1)} %get-tuple-element.7, ...), kind=kLoop, calls=%fused_computation | loop fusion | flops 6144 | bytes 36864 | tf_op jit(solution)/shard_map/add | solution.py:346
Async XLA Ops:
  0.6 0.7 %copy-start = (f32[64]{0:T(128)S(1)}, f32[64]{0:T(128)}, u32[]{:S(2)}) copy-start(f32[64]{0:T(128)} %param.7) | copy-start | bytes 772
  0.6 0.7 %copy-start.1 = (f32[64]{0:T(128)S(1)}, f32[64]{0:T(128)}, u32[]{:S(2)}) copy-start(f32[64]{0:T(128)} %param.8) | copy-start | bytes 772
  1.3 42.6 %copy-start.2 = (f32[16,64]{1,0:T(8,128)S(1)}, f32[16,64]{1,0:T(8,128)}, u32[]{:S(2)}) copy-start(f32[16,64]{1,0:T(8,128)} %residual_hbm.1) | copy-start | bytes 12292
  1.3 42.6 %copy-start.3 = (f32[16,64]{1,0:T(8,128)S(1)}, f32[16,64]{1,0:T(8,128)}, u32[]{:S(2)}) copy-start(f32[16,64]{1,0:T(8,128)} %direction_hbm.1) | copy-start | bytes 12292
  1.3 42.6 %copy-start.4 = (f32[16,64]{1,0:T(8,128)S(1)}, f32[16,64]{1,0:T(8,128)}, u32[]{:S(2)}) copy-start(f32[16,64]{1,0:T(8,128)} %param.9) | copy-start | bytes 12292

commit v5 on v4

--- a/solution.py
+++ b/solution.py
@@ -335,13 +335,13 @@
             dma((ny, 2)), dma, dma, dma, dma, dma,
         ],
         compiler_params=pltpu.CompilerParams(
-            collective_id=0, has_side_effects=True, vmem_limit_bytes=539 * 1024 * 1024 // 10),
+            collective_id=0, has_side_effects=True, vmem_limit_bytes=32 * 1024 * 1024),
         name="cg_step",
     )
 
     def on_device(points, lengthscale, noise, iterate, residual, direction):
-        image, alpha, beta = step(
-            points, lengthscale.reshape(1, FEAT), noise.reshape(1, PTS), residual, direction)
+        operands = (points, lengthscale.reshape(1, FEAT), noise.reshape(1, PTS), residual, direction)
+        image, alpha, beta = step(*(pltpu.with_memory_space_constraint(a, pltpu.HBM) for a in operands))
         fresh = residual - alpha * image
         return iterate + alpha * direction, fresh, fresh + beta * direction
 

time: 44.8 us -> 44.1 us (0.984)
  local copies, waits for them, and re-layouts: 0.67 us -> 0.01 us
    unnamed x10 -> x6, local copies, waits for them, and re-layouts: 0.67 us -> 0.01 us
where the time goes in v5:
time: 44.1 us; the launch traced here: 43.9 us
  Pallas kernels  42.6 us (97%)
  between operations  0.69 us (2%)
  other arithmetic  0.61 us (1%)
    pallas_call x1, Pallas kernels, on_device(): step(*(pltpu.with_memory_space_constraint(a, pltpu.HBM) for a in operands))  42.6 us

profile of v5, /device:TPU:1, one launch (start us, length us, event | category | flops | bytes accessed | tf_op | source)
XLA Modules:
  0.0 43.9 jit_solution(1728592812322856032)
XLA Ops:
  0.6 0.0 copy-start
  0.6 0.0 copy-start.1
  0.7 0.0 copy-start.2
  0.7 42.6 %cg_step.1 = (f32[16,64]{1,0:T(8,128)S(1)}, f32[16,64]{1,0:T(8,128)S(1)}, f32[16,64]{1,0:T(8,128)S(1)}) custom-call(f32[64,64]{1,0:T(8,128)} %points_hbm.1, f32[1,64]{1,0:T(1,128)} %bitcast.2, f32[1,64]{1,0:T(1,128)} %bitcast.3, f32[16,64]{1,0:T(8,128)} %residual_hbm.1, f32[16,64]{1,0:T(8,128)} %direction_hbm.1), custom_call_target="tpu_custom_call" | custom-call | tf_op jit(solution)/shard_map/cg_step/pallas_call | solution.py:344
  43.3 0.0 copy-done
  43.3 0.0 copy-done.1
  43.3 0.0 copy-done.2
  43.3 0.6 %multiply_add_fusion = (f32[16,64]{1,0:T(8,128)}, f32[16,64]{1,0:T(8,128)}, f32[16,64]{1,0:T(8,128)}) fusion(f32[16,64]{1,0:T(8,128)S(1)} %get-tuple-element.8, f32[16,64]{1,0:T(8,128)S(1)} %copy-done.1, f32[16,64]{1,0:T(8,128)S(1)} %copy-done, f32[16,64]{1,0:T(8,128)S(1)} %get-tuple-element.6, f32[16,64]{1,0:T(8,128)S(1)} %get-tuple-element.7, ...), kind=kLoop, calls=%fused_computation | loop fusion | flops 6144 | bytes 36864 | tf_op jit(solution)/shard_map/add | solution.py:346
Async XLA Ops:
  0.6 42.7 %copy-start = (f32[16,64]{1,0:T(8,128)S(1)}, f32[16,64]{1,0:T(8,128)}, u32[]{:S(2)}) copy-start(f32[16,64]{1,0:T(8,128)} %residual_hbm.1) | copy-start | bytes 12292
  0.6 42.7 %copy-start.1 = (f32[16,64]{1,0:T(8,128)S(1)}, f32[16,64]{1,0:T(8,128)}, u32[]{:S(2)}) copy-start(f32[16,64]{1,0:T(8,128)} %direction_hbm.1) | copy-start | bytes 12292
  0.7 42.7 %copy-start.2 = (f32[16,64]{1,0:T(8,128)S(1)}, f32[16,64]{1,0:T(8,128)}, u32[]{:S(2)}) copy-start(f32[16,64]{1,0:T(8,128)} %param.9) | copy-start | bytes 12292

commit v6 on v5

--- a/solution.py
+++ b/solution.py
@@ -250,9 +250,11 @@
     loads[3].wait()
     loads[4].wait()
     res = residual[...]
+    rr_own = jnp.sum(res * res, axis=1, keepdims=True)
+    damped = noise[...] * own_dir
     arrived(pbuf.at[pl.ds(1, nrow - 1)], p_recv)
     total = jnp.sum(pbuf[...], axis=0)
-    image = jnp.concatenate([total, swap(total)], axis=0)[:, 0:64] + noise[...] * own_dir
+    image = jnp.concatenate([total, swap(total)], axis=0)[:, 0:64] + damped
     image_out[...] = image
 
     def norm(a, b):
@@ -260,7 +262,7 @@
 
     sub16s = lax.broadcasted_iota(jnp.int32, (16, 128), 0)
     stats8 = jnp.where(
-        lane16 == 4 * sub16s, norm(res, res),
+        lane16 == 4 * sub16s, rr_own,
         jnp.where(lane16 == 4 * sub16s + 1, norm(own_dir, image),
                   jnp.where(lane16 == 4 * sub16s + 2, norm(res, image),
                             jnp.where(lane16 == 4 * sub16s + 3, norm(image, image), 0.0))))

time: 44.1 us -> 44.1 us (level)
  no operation moved by 1% of the time
where the time goes in v6:
time: 44.1 us; the launch traced here: 43.9 us
  Pallas kernels  42.6 us (97%)
  between operations  0.69 us (2%)
  other arithmetic  0.61 us (1%)
    pallas_call x1, Pallas kernels, on_device(): step(*(pltpu.with_memory_space_constraint(a, pltpu.HBM) for a in operands))  42.6 us

profile of v6, /device:TPU:1, one launch (start us, length us, event | category | flops | bytes accessed | tf_op | source)
XLA Modules:
  0.0 43.9 jit_solution(5293694809112045480)
XLA Ops:
  0.6 0.0 copy-start
  0.6 0.0 copy-start.1
  0.7 0.0 copy-start.2
  0.7 42.6 %cg_step.1 = (f32[16,64]{1,0:T(8,128)S(1)}, f32[16,64]{1,0:T(8,128)S(1)}, f32[16,64]{1,0:T(8,128)S(1)}) custom-call(f32[64,64]{1,0:T(8,128)} %points_hbm.1, f32[1,64]{1,0:T(1,128)} %bitcast.2, f32[1,64]{1,0:T(1,128)} %bitcast.3, f32[16,64]{1,0:T(8,128)} %residual_hbm.1, f32[16,64]{1,0:T(8,128)} %direction_hbm.1), custom_call_target="tpu_custom_call" | custom-call | tf_op jit(solution)/shard_map/cg_step/pallas_call | solution.py:346
  43.3 0.0 copy-done
  43.3 0.0 copy-done.1
  43.3 0.0 copy-done.2
  43.3 0.6 %multiply_add_fusion = (f32[16,64]{1,0:T(8,128)}, f32[16,64]{1,0:T(8,128)}, f32[16,64]{1,0:T(8,128)}) fusion(f32[16,64]{1,0:T(8,128)S(1)} %get-tuple-element.8, f32[16,64]{1,0:T(8,128)S(1)} %copy-done.1, f32[16,64]{1,0:T(8,128)S(1)} %copy-done, f32[16,64]{1,0:T(8,128)S(1)} %get-tuple-element.6, f32[16,64]{1,0:T(8,128)S(1)} %get-tuple-element.7, ...), kind=kLoop, calls=%fused_computation | loop fusion | flops 6144 | bytes 36864 | tf_op jit(solution)/shard_map/add | solution.py:348
Async XLA Ops:
  0.6 42.6 %copy-start = (f32[16,64]{1,0:T(8,128)S(1)}, f32[16,64]{1,0:T(8,128)}, u32[]{:S(2)}) copy-start(f32[16,64]{1,0:T(8,128)} %residual_hbm.1) | copy-start | bytes 12292
  0.6 42.6 %copy-start.1 = (f32[16,64]{1,0:T(8,128)S(1)}, f32[16,64]{1,0:T(8,128)}, u32[]{:S(2)}) copy-start(f32[16,64]{1,0:T(8,128)} %direction_hbm.1) | copy-start | bytes 12292
  0.7 42.6 %copy-start.2 = (f32[16,64]{1,0:T(8,128)S(1)}, f32[16,64]{1,0:T(8,128)}, u32[]{:S(2)}) copy-start(f32[16,64]{1,0:T(8,128)} %param.9) | copy-start | bytes 12292
